TPU v7x, 32 devices: a whole 2x2x4 slice. The times are simulated.
32 devices in a mesh: rep: 4 (over x, core), fsdp: 8 (over z, y).
Axes of the slice: x: 2, y: 2, z: 4, core: 2. Of those that a mesh axis runs over, the one named last changes fastest.
Arguments:
- acts: bfloat16 [4, 2048, 8192], P('rep', 'fsdp'), may hold values from -6 to 6
- out_grad: bfloat16 [4, 2048, 512], P('rep', 'fsdp'), may hold values from -6 to 6
- weights: bfloat16 [4, 8192, 512], P('rep', 'fsdp'), may hold values from -0.0625 to 0.0625
- anchor: float32 [8192, 512], P('fsdp', 'rep'), may hold values from -0.0625 to 0.0625
- momentum: float32 [8192, 512], P('fsdp', 'rep'), may hold values from -0.078125 to 0.078125
- plan: int32 [4], replicated, may hold values 0 or 1
Outputs:
- values: bfloat16 [4, 2048, 512], P('rep', 'fsdp')
- act_grad: bfloat16 [4, 2048, 8192], P('rep', 'fsdp')
- new_weights: bfloat16 [4, 8192, 512], P('rep', 'fsdp')
- new_momentum: float32 [8192, 512], P('fsdp', 'rep')
All inputs are finite; a program needn't handle non-finite values.
Results may differ from a plain program's by a relative error of at most 0.001.
Values may be sent and summed in bfloat16 or wider, within the bound.
A program may use at most 128 MiB of HBM per device.

v0:
```python
import math

import jax
import jax.numpy as jnp
from jax import lax
from jax.sharding import PartitionSpec as P

outer_rate = 0.7
momentum_coef = 0.9


def local(acts, out_grad, weights, anchor, momentum, plan):
    tokens = acts[0]
    grads_out = out_grad[0]
    local_weight = weights[0]
    total_tokens = tokens.shape[0] * lax.axis_size("fsdp")
    inner_rate = 1.0 / math.sqrt(total_tokens * tokens.shape[1])
    full_weight = lax.all_gather(local_weight, "fsdp", axis=0, tiled=True)
    values = jnp.dot(tokens, full_weight, preferred_element_type=jnp.float32).astype(jnp.bfloat16)
    act_grad = lax.dot_general(
        grads_out, full_weight, (((1,), (1,)), ((), ())), preferred_element_type=jnp.float32
    ).astype(jnp.bfloat16)
    weight_grad = lax.psum_scatter(
        lax.dot_general(
            tokens, grads_out, (((0,), (0,)), ((), ())), preferred_element_type=jnp.float32
        ),
        "fsdp",
        scatter_dimension=0,
        tiled=True,
    )
    inner_weight = local_weight.astype(jnp.float32) - inner_rate * weight_grad
    head_dim = local_weight.shape[1] // plan.shape[0]
    col_mask = jnp.repeat(plan, head_dim) > 0
    block_width = anchor.shape[1]
    offset = lax.axis_index("rep") * block_width
    group_count = lax.axis_size("rep")
    group_total = lax.psum(inner_weight, "rep")
    mom_all, anchor_all = (
        lax.all_gather(momentum, "rep", axis=1, tiled=True),
        lax.all_gather(anchor, "rep", axis=1, tiled=True),
    )
    group_mean = group_total / group_count
    pseudo_grad = anchor_all - group_mean
    mom_full = momentum_coef * mom_all + pseudo_grad
    outer_all = (anchor_all - outer_rate * (pseudo_grad + momentum_coef * mom_full)).astype(
        jnp.bfloat16
    )
    mom_next = lax.dynamic_slice_in_dim(mom_full, offset, block_width, 1)
    block_mask = lax.dynamic_slice_in_dim(col_mask, offset, block_width, 0)
    new_weight = jnp.where(col_mask[None, :], outer_all, inner_weight.astype(jnp.bfloat16))
    new_momentum = jnp.where(block_mask[None, :], mom_next, momentum)
    return (values[None], act_grad[None], new_weight[None], new_momentum)


def solution(mesh):
    placed = (
        P("rep", "fsdp", None),
        P("rep", "fsdp", None),
        P("rep", "fsdp", None),
        P("fsdp", "rep"),
        P("fsdp", "rep"),
        P(),
    )
    return jax.shard_map(
        local,
        mesh=mesh,
        in_specs=placed,
        out_specs=(
            P("rep", "fsdp", None),
            P("rep", "fsdp", None),
            P("rep", "fsdp", None),
            P("fsdp", "rep"),
        ),
        check_vma=False,
    )
```

profile of v0, /device:TPU:13, one launch (start us, length us, event | category | flops | bytes accessed | tf_op | source)
XLA Modules:
  0.0 543.7 jit_solution(14627476526137463271)
XLA Ops:
  7.2 0.0 copy-start
  7.2 0.0 reduce-scatter.2.cloned.1.call-start
  7.2 0.9 copy-done
  8.1 10.3 %fusion.4 = f32[8192,512]{1,0:T(8,128)} fusion(bf16[1,256,8192]{2,1,0:T(8,128)(2,1)} %param.6, bf16[1,256,512]{2,1,0:T(8,128)(2,1)S(1)} %copy-done), kind=kOutput, calls=%fused_computation.5 | convolution fusion | flops 2147483648 | bytes 21233664 | tf_op jit(solution)/shard_map/dot_general | solution.py:24
  18.4 0.0 reduce-scatter.2.cloned.1.call-update
  18.5 0.0 copy-start.9
  18.5 0.0 copy-start.6
  18.5 0.0 all-gather.9.cloned.1.call-start
  18.5 0.7 all-gather.9.cloned.1.call-update
  19.2 0.0 all-gather.5.cloned.1.call-start
  19.3 0.7 all-gather.5.cloned.1.call-update
  20.0 0.0 all-gather.7.cloned.1.call-start
  20.0 0.5 all-gather.7.cloned.1.call-update
  20.5 0.0 all-reduce.2.cloned.1.call-start
  20.6 0.0 copy-done.9
  20.6 0.1 broadcast_bitcast_fusion
  20.7 0.1 dynamic_slice.6
  20.8 279.9 %reduce-scatter.2.cloned.1.call-done = f32[1024,512]{1,0:T(8,128)} async-done(((f32[8192,512]{1,0:T(8,128)}), f32[1024,512]{1,0:T(8,128)}) %reduce-scatter.2.cloned.1.call-update) | async-done | bytes 2097168 | tf_op jit(solution)/shard_map/reduce_scatter | solution.py:23
  300.7 0.0 copy-done.6
  300.7 3.2 convert_subtract_fusion
  304.0 0.0 all-reduce.2.cloned.1.call-update
  304.0 121.8 %all-gather.9.cloned.1.call-done = bf16[1,8192,512]{2,1,0:T(8,128)(2,1)} async-done(((bf16[1,1024,512]{2,1,0:T(8,128)(2,1)}), bf16[1,8192,512]{2,1,0:T(8,128)(2,1)}) %all-gather.9.cloned.1.call-update) | async-done | bytes 8388624 | tf_op jit(solution)/shard_map/all_gather | solution.py:18
  425.8 0.0 copy-start.2
  425.8 0.0 copy-start.7
  425.8 7.9 %fusion = bf16[1,256,8192]{2,1,0:T(8,128)(2,1)} fusion(bf16[1,8192,512]{2,1,0:T(8,128)(2,1)} %all-gather.9.cloned.1.call-done, bf16[1,256,512]{2,1,0:T(8,128)(2,1)S(1)} %copy-done), kind=kOutput, calls=%fused_computation.1 | convolution fusion | flops 2149580800 | bytes 12845056 | tf_op jit(solution)/shard_map/dot_general | solution.py:20
  433.7 0.0 copy-done.2
  433.7 0.0 copy-done.7
  433.7 3.0 fusion.12
  436.7 0.0 copy-start.8
  436.7 15.2 %all-gather.5.cloned.1.call-done = f32[1024,512]{1,0:T(8,128)} async-done(((f32[1024,128]{1,0:T(8,128)}), f32[1024,512]{1,0:T(8,128)}) %all-gather.5.cloned.1.call-update) | async-done | bytes 2097168 | tf_op jit(solution)/shard_map/all_gather | solution.py:40
  451.9 24.4 %all-gather.7.cloned.1.call-done = f32[1024,512]{1,0:T(8,128)} async-done(((f32[1024,128]{1,0:T(8,128)}), f32[1024,512]{1,0:T(8,128)}) %all-gather.7.cloned.1.call-update) | async-done | bytes 2097168 | tf_op jit(solution)/shard_map/all_gather | solution.py:39
  476.3 53.3 %all-reduce.2.cloned.1.call-done = f32[1024,512]{1,0:T(8,128)} async-done(((f32[1024,512]{1,0:T(8,128)}), f32[1024,512]{1,0:T(8,128)}) %all-reduce.2.cloned.1.call-update) | async-done | bytes 2097168 | tf_op jit(solution)/shard_map/psum | solution.py:37
  529.6 0.0 copy-start.1
  529.6 0.0 copy-start.3
  529.6 0.0 copy-start.4
  529.6 0.0 copy-start.5
  529.6 3.8 multiply_add_fusion
  533.4 0.0 copy-done.8
  533.4 0.9 dynamic-slice_select_fusion
  534.3 0.0 copy-done.1
  534.3 0.0 copy-done.3
  534.3 0.0 copy-done.4
  534.3 0.8 copy-done.5
  535.1 2.1 fusion.18
  (1 shorter events, 0.0 us)
Async XLA Ops:
  7.2 1.0 copy-start
  7.2 293.5 %reduce-scatter.2.cloned.1.call-start = ((), (), s32[]{:S(2)}) async-start(), calls=%async_computation.2 | async-start | bytes 18874368 | tf_op jit(solution)/shard_map/reduce_scatter | solution.py:23
  18.5 2.1 copy-start.9
  18.5 282.2 %copy-start.6 = (bf16[1,1024,512]{2,1,0:T(8,128)(2,1)S(1)}, bf16[1,1024,512]{2,1,0:T(8,128)(2,1)}, u32[]{:S(2)}) copy-start(bf16[1,1024,512]{2,1,0:T(8,128)(2,1)} %param.8) | copy-start | bytes 3145732
  18.5 407.3 %all-gather.9.cloned.1.call-start = ((), (), s32[]{:S(2)}) async-start(), calls=%async_computation.5 | async-start | bytes 9437184 | tf_op jit(solution)/shard_map/all_gather | solution.py:18
  19.2 432.7 %all-gather.5.cloned.1.call-start = ((), (), s32[]{:S(2)}) async-start(), calls=%async_computation.1 | async-start | bytes 2621440 | tf_op jit(solution)/shard_map/all_gather | solution.py:40
  20.0 456.3 %all-gather.7.cloned.1.call-start = ((), (), s32[]{:S(2)}) async-start(), calls=%async_computation.4 | async-start | bytes 2621440 | tf_op jit(solution)/shard_map/all_gather | solution.py:39
  20.5 509.0 %all-reduce.2.cloned.1.call-start = ((), (), s32[]{:S(2)}) async-start(), calls=%async_computation.3 | async-start | bytes 4194304 | tf_op jit(solution)/shard_map/psum | solution.py:37
  425.8 7.9 %copy-start.2 = (bf16[1,8192,512]{2,1,0:T(8,128)(2,1)S(1)}, bf16[1,8192,512]{2,1,0:T(8,128)(2,1)}, u32[]{:S(2)}) copy-start(bf16[1,8192,512]{2,1,0:T(8,128)(2,1)} %all-gather.9.cloned.1.call-done) | copy-start | bytes 25165828
  425.8 7.9 %copy-start.7 = (bf16[1,256,8192]{2,1,0:T(8,128)(2,1)S(1)}, bf16[1,256,8192]{2,1,0:T(8,128)(2,1)}, u32[]{:S(2)}) copy-start(bf16[1,256,8192]{2,1,0:T(8,128)(2,1)} %param.6) | copy-start | bytes 12582916
  436.7 96.7 %copy-start.8 = (f32[1024,128]{1,0:T(8,128)S(1)}, f32[1024,128]{1,0:T(8,128)}, u32[]{:S(2)}) copy-start(f32[1024,128]{1,0:T(8,128)} %param.10) | copy-start | bytes 1572868
  529.6 4.7 copy-start.1
  529.6 4.7 copy-start.3
  529.6 4.7 copy-start.4
  529.6 5.5 %copy-start.5 = (f32[1024,512]{1,0:T(8,128)S(1)}, f32[1024,512]{1,0:T(8,128)}, u32[]{:S(2)}) copy-start(f32[1024,512]{1,0:T(8,128)} %all-reduce.2.cloned.1.call-done) | copy-start | bytes 6291460
Sparse Core Ops, SparseCore 0:
  18.6 282.0 reduce-scatter.1
  303.1 122.6 all-gather.8
  427.4 24.4 all-gather.4
  453.4 22.8 all-gather.6
  478.6 50.8 all-reduce.1
where the time goes:
time: 546 us; the launch traced here: 544 us
  waiting for transfers between devices  496 us (91%)
  matrix products  21.3 us (4%)
  between operations  13.8 us (3%)
  other arithmetic  10.1 us (2%)
    reduce_scatter x1, waiting for transfers between devices, local(): lax.psum_scatter(lax.dot_general(tokens, grads_out, (((0,), (0,)), ((), (...  280 us
    all_gather x1, waiting for transfers between devices, local(): full_weight = lax.all_gather(local_weight, 'fsdp', axis=0, tiled=True)  122 us
    psum x1, waiting for transfers between devices, local(): group_total = lax.psum(inner_weight, 'rep')  53.3 us
    all_gather x1, waiting for transfers between devices, local(): lax.all_gather(momentum, 'rep', axis=1, tiled=True)  24.4 us
    all_gather x1, waiting for transfers between devices, local(): lax.all_gather(anchor, 'rep', axis=1, tiled=True)  15.2 us
  transfers between devices with their start and end apart: 5, of which 5 were waited for; matrix products, arithmetic and copies ran while one was open for 3% of the time, Pallas kernels for 0%

commit v1 on v0

v1 whole, which is shorter than its diff:
```python
import functools
import math

import jax
import jax.numpy as jnp
from jax import lax
from jax.experimental import pallas as pl
from jax.experimental.pallas import tpu as pltpu
from jax.sharding import PartitionSpec as P

outer_rate = 0.7
momentum_coef = 0.9
MESH = pl.DeviceIdType.MESH
F32 = jnp.float32
BF16 = jnp.bfloat16
LEFT, RIGHT, PARTNER = 0, 1, 2


def kernel(
    n, groups, chunks, rate,
    plan, acts_hbm, og_hbm, w_hbm, anchor_hbm, mom_hbm,
    values_out, ag_hbm, new_w_out, new_mom_out,
    acts, acts_t, og_all, w_all, ag, vals, wgrad, inner, rep_in, outer_in, anchor, mom,
    acts_sem, og_sem, w_sem, state_sem, ag_sem,
    og_send, og_recv, w_send, w_recv, a_send, a_recv,
    r_send, r_recv, o_send, o_recv,
):
    me = lax.axis_index("fsdp")
    rep = lax.axis_index("rep")
    line = n // 2
    z = me // 2
    y = lax.rem(me, 2)
    width = acts.shape[2]
    rows = w_all.shape[2]
    block = anchor.shape[1]

    def cols(s):
        return pl.ds(pl.multiple_of(s * width, width), width)

    def load_acts(s):
        return pltpu.make_async_copy(acts_hbm.at[:, cols(s)], acts.at[s], acts_sem.at[s])

    def load_w(c):
        return pltpu.make_async_copy(
            w_hbm.at[pl.ds(c * rows, rows)], w_all.at[me, c], w_sem.at[c]
        )

    load_og = pltpu.make_async_copy(og_hbm, og_all.at[me], og_sem.at[0])
    load_anchor = pltpu.make_async_copy(anchor_hbm, anchor, state_sem.at[0])
    load_mom = pltpu.make_async_copy(mom_hbm, mom, state_sem.at[1])
    load_og.start()
    for c in range(chunks):
        load_w(c).start()

    @pl.loop(0, n)
    def _(s):
        load_acts(s).start()

    load_anchor.start()
    load_mom.start()

    barrier = pltpu.get_barrier_semaphore()

    @pl.loop(1, n)
    def _(k):
        pl.semaphore_signal(
            barrier, inc=1, device_id={"fsdp": lax.rem(me + k, n)}, device_id_type=MESH
        )

    @pl.loop(1, groups)
    def _(k):
        pl.semaphore_signal(
            barrier, inc=1, device_id={"rep": lax.rem(rep + k, groups)}, device_id_type=MESH
        )

    pl.semaphore_wait(barrier, n - 1 + groups - 1)

    def target(way):
        return (jnp.maximum(me - 2, 0), jnp.minimum(me + 2, n - 1), me + 1 - 2 * y)[way]

    def og_copy(s, way):
        return pltpu.make_async_remote_copy(
            src_ref=og_all.at[s], dst_ref=og_all.at[s],
            send_sem=og_send.at[s, way], recv_sem=og_recv.at[s],
            device_id={"fsdp": target(way)}, device_id_type=MESH,
        )

    def w_copy(c):
        def make(s, way):
            return pltpu.make_async_remote_copy(
                src_ref=w_all.at[s, c], dst_ref=w_all.at[s, c],
                send_sem=w_send.at[s, c, way], recv_sem=w_recv.at[s, c],
                device_id={"fsdp": target(way)}, device_id_type=MESH,
            )
        return make

    def own(make, act):
        s = me
        pl.when(z > 0)(lambda: act(make(s, LEFT)))
        pl.when(z < line - 1)(lambda: act(make(s, RIGHT)))
        act(make(s, PARTNER))

    def forward(make, k, act, wait):
        @pl.when(z >= k)
        def _():
            s = me - 2 * k
            if wait:
                make(s, PARTNER).wait_recv()
            pl.when(z < line - 1)(lambda: act(make(s, RIGHT)))
            act(make(s, PARTNER))

        @pl.when(z + k < line)
        def _():
            s = me + 2 * k
            if wait:
                make(s, PARTNER).wait_recv()
            pl.when(z > 0)(lambda: act(make(s, LEFT)))
            act(make(s, PARTNER))

    def start(copy):
        copy.start()

    def wait_send(copy):
        copy.wait_send()

    def a_copy(k):
        d = lax.rem(me + k, n)
        return pltpu.make_async_remote_copy(
            src_ref=acts_hbm.at[:, cols(d)], dst_ref=acts_t.at[me],
            send_sem=a_send.at[k], recv_sem=a_recv.at[me],
            device_id={"fsdp": d}, device_id_type=MESH,
        )

    def a_arrived(s):
        return pltpu.make_async_remote_copy(
            src_ref=acts_hbm.at[:, cols(s)], dst_ref=acts_t.at[s],
            send_sem=a_send.at[0], recv_sem=a_recv.at[s],
            device_id={"fsdp": lax.rem(me + 1, n)}, device_id_type=MESH,
        )

    load_og.wait()
    own(og_copy, start)

    @pl.loop(1, n)
    def _(k):
        a_copy(k).start()

    for c in range(chunks):
        load_w(c).wait()
        own(w_copy(c), start)

    def ag_store(s):
        return pltpu.make_async_copy(ag.at[s], ag_hbm.at[:, cols(s)], ag_sem.at[s])

    def use_weight(s):
        for c in range(chunks):
            part = slice(c * rows, (c + 1) * rows)
            vals[...] += jnp.dot(acts[s, :, part], w_all[s, c], preferred_element_type=F32)
            ag[s, :, part] = lax.dot_general(
                og_all[me], w_all[s, c], (((1,), (1,)), ((), ())), preferred_element_type=F32
            ).astype(BF16)
        ag_store(s).start()

    def use_acts(a, s):
        wgrad[...] += lax.dot_general(
            a, og_all[s], (((0,), (0,)), ((), ())), preferred_element_type=F32
        )

    vals[...] = jnp.zeros_like(vals)
    wgrad[...] = jnp.zeros_like(wgrad)

    @pl.loop(0, n)
    def _(s):
        load_acts(s).wait()

    @pl.loop(1, line)
    def _(k):
        forward(og_copy, k, start, True)

    use_weight(me)
    use_acts(acts[me], me)

    def gather(k):
        for c in range(chunks):
            forward(w_copy(c), k, start, True)

    def use_line(k):
        @pl.loop(0, 2)
        def _(j):
            zz = z + (1 - 2 * j) * k

            @pl.when((zz >= 0) & (zz < line))
            def _():
                use_weight(zz * 2 + y)

    def use_partner(k):
        @pl.loop(0, 2)
        def _(j):
            zz = z + (1 - 2 * j) * k

            @pl.when((zz >= 0) & (zz < line) & ((k > 0) | (j == 0)))
            def _():
                s = zz * 2 + 1 - y
                for c in range(chunks):
                    w_copy(c)(s, PARTNER).wait_recv()
                use_weight(s)

    gather(1)

    @pl.loop(0, line)
    def _(zz):
        og_copy(zz * 2 + 1 - y, PARTNER).wait_recv()

    @pl.loop(1, n)
    def _(k):
        s = lax.rem(me + n - k, n)
        a_arrived(s).wait_recv()
        use_acts(acts_t[s], s)

    for j in range(groups):
        part = slice(j * block, (j + 1) * block)
        for c in range(chunks):
            across = slice(c * rows, (c + 1) * rows)
            inner[j, across] = (
                w_all[me, c, :, part].astype(F32) - rate * wgrad[across, part]
            )

    def r_copy(k):
        d = lax.rem(rep + k, groups)
        return pltpu.make_async_remote_copy(
            src_ref=inner.at[d], dst_ref=rep_in.at[rep],
            send_sem=r_send.at[k], recv_sem=r_recv.at[rep],
            device_id={"rep": d}, device_id_type=MESH,
        )

    def r_arrived(k):
        d = lax.rem(rep + k, groups)
        return pltpu.make_async_remote_copy(
            src_ref=inner.at[d], dst_ref=rep_in.at[d],
            send_sem=r_send.at[k], recv_sem=r_recv.at[d],
            device_id={"rep": d}, device_id_type=MESH,
        )

    def o_copy(k):
        d = lax.rem(rep + k, groups)
        return pltpu.make_async_remote_copy(
            src_ref=outer_in.at[rep], dst_ref=outer_in.at[rep],
            send_sem=o_send.at[k], recv_sem=o_recv.at[rep],
            device_id={"rep": d}, device_id_type=MESH,
        )

    def o_arrived(k):
        d = lax.rem(rep + k, groups)
        return pltpu.make_async_remote_copy(
            src_ref=outer_in.at[d], dst_ref=outer_in.at[d],
            send_sem=o_send.at[k], recv_sem=o_recv.at[d],
            device_id={"rep": d}, device_id_type=MESH,
        )

    for k in range(1, groups):
        r_copy(k).start()
    rep_in[rep] = inner[rep]

    use_line(1)
    use_partner(0)

    @pl.loop(2, line)
    def _(k):
        gather(k)
        use_line(k)
        use_partner(k - 1)

    for k in range(1, groups):
        r_arrived(k).wait_recv()
    load_anchor.wait()
    load_mom.wait()
    total = rep_in[0]
    for j in range(1, groups):
        total = total + rep_in[j]
    pseudo_grad = anchor[...] - total / groups
    mom_next = momentum_coef * mom[...] + pseudo_grad
    outer_in[rep] = (
        anchor[...] - outer_rate * (pseudo_grad + momentum_coef * mom_next)
    ).astype(BF16)
    for k in range(1, groups):
        o_copy(k).start()
    synced = jnp.full(mom_next.shape, plan[rep], jnp.int32) > 0
    new_mom_out[...] = jnp.where(synced, mom_next, mom[...])

    use_partner(line - 1)
    values_out[...] = vals[...].astype(BF16)

    for k in range(1, groups):
        o_arrived(k).wait_recv()
    for j in range(groups):
        synced = jnp.full(inner.shape[1:], plan[j], jnp.int32) > 0
        new_w_out[:, j * block:(j + 1) * block] = jnp.where(
            synced, outer_in[j].astype(F32), inner[j]
        ).astype(BF16)

    own(og_copy, wait_send)
    for c in range(chunks):
        own(w_copy(c), wait_send)

    @pl.loop(1, line)
    def _(k):
        forward(og_copy, k, wait_send, False)
        for c in range(chunks):
            forward(w_copy(c), k, wait_send, False)

    @pl.loop(1, n)
    def _(k):
        a_copy(k).wait_send()

    for k in range(1, groups):
        r_copy(k).wait_send()
        o_copy(k).wait_send()

    @pl.loop(0, n)
    def _(s):
        ag_store(s).wait()


def local(n, groups, acts, out_grad, weights, anchor, momentum, plan):
    tokens, depth = acts.shape[1:]
    rows, kvw = weights.shape[1:]
    block = anchor.shape[1]
    rate = 1.0 / math.sqrt(tokens * n * depth)
    chunks = 2
    any_spec = pl.BlockSpec(memory_space=pl.ANY)
    vmem = pl.BlockSpec(memory_space=pltpu.VMEM)
    dma = pltpu.SemaphoreType.DMA
    values, act_grad, new_w, new_mom = pl.pallas_call(
        functools.partial(kernel, n, groups, chunks, rate),
        out_shape=(
            jax.ShapeDtypeStruct((tokens, kvw), BF16),
            jax.ShapeDtypeStruct((tokens, depth), BF16),
            jax.ShapeDtypeStruct((rows, kvw), BF16),
            jax.ShapeDtypeStruct((rows, block), F32),
        ),
        in_specs=[pl.BlockSpec(memory_space=pltpu.SMEM)] + [any_spec] * 5,
        out_specs=(vmem, any_spec, vmem, vmem),
        scratch_shapes=[
            pltpu.VMEM((n, tokens, rows), BF16),
            pltpu.VMEM((n, tokens, rows), BF16),
            pltpu.VMEM((n, tokens, kvw), BF16),
            pltpu.VMEM((n, chunks, rows // chunks, kvw), BF16),
            pltpu.VMEM((n, tokens, rows), BF16),
            pltpu.VMEM((tokens, kvw), F32),
            pltpu.VMEM((rows, kvw), F32),
            pltpu.VMEM((groups, rows, block), F32),
            pltpu.VMEM((groups, rows, block), F32),
            pltpu.VMEM((groups, rows, block), BF16),
            pltpu.VMEM((rows, block), F32),
            pltpu.VMEM((rows, block), F32),
            dma((n,)), dma((1,)), dma((chunks,)), dma((2,)), dma((n,)),
            dma((n, 3)), dma((n,)), dma((n, chunks, 3)), dma((n, chunks)), dma((n,)), dma((n,)),
            dma((groups,)), dma((groups,)), dma((groups,)), dma((groups,)),
        ],
        compiler_params=pltpu.CompilerParams(
            collective_id=0, has_side_effects=True, vmem_limit_bytes=56 * 2**20
        ),
        cost_estimate=pl.CostEstimate(
            flops=6 * tokens * depth * kvw, bytes_accessed=24 * 2**20, transcendentals=0
        ),
    )(plan, acts[0], out_grad[0], weights[0], anchor, momentum)
    return values[None], act_grad[None], new_w[None], new_mom


def solution(mesh):
    placed = (
        P("rep", "fsdp", None),
        P("rep", "fsdp", None),
        P("rep", "fsdp", None),
        P("fsdp", "rep"),
        P("fsdp", "rep"),
        P(),
    )
    return jax.shard_map(
        functools.partial(local, mesh.shape["fsdp"], mesh.shape["rep"]),
        mesh=mesh,
        in_specs=placed,
        out_specs=(
            P("rep", "fsdp", None),
            P("rep", "fsdp", None),
            P("rep", "fsdp", None),
            P("fsdp", "rep"),
        ),
        check_vma=False,
    )
```

time: 546 us -> 228 us (0.42)
  waiting for transfers between devices: 496 us -> 0 us
  Pallas kernels: 0 us -> 218 us
  matrix products: 21.3 us -> 0 us
  between operations: 13.8 us -> 0.64 us
  other arithmetic: 10.1 us -> 0 us
  local copies, waits for them, and re-layouts: 1.87 us -> 8.2 us
    reduce_scatter x1 -> x0, waiting for transfers between devices: 280 us -> none  [local(): lax.psum_scatter(lax.dot_general(tokens, grads_out, (((0,), (0,)), ((), (...]
    pallas_call x0 -> x1, Pallas kernels: none -> 218 us  [local(): pl.pallas_call(functools.partial(kernel, n, groups, chunks, rate), out_sh...]
    all_gather x3 -> x0, waiting for transfers between devices: 161 us -> none  [the longest x1 122 us: local(): full_weight = lax.all_gather(local_weight, 'fsdp', axis=0, tiled=True)]
    psum x1 -> x0, waiting for transfers between devices: 53.3 us -> none  [local(): group_total = lax.psum(inner_weight, 'rep')]
    dot_general x3 -> x0, matrix products: 21.3 us -> none  [the longest x1 10.3 us: local(): lax.dot_general(tokens, grads_out, (((0,), (0,)), ((), ())), preferred_el...]
    unnamed x20 -> x8, local copies, waits for them, and re-layouts: 1.72 us -> 8.2 us
  transfers between devices with their start and end apart: 5 -> 0, of which waited for: 5 -> 0; matrix products, arithmetic and copies ran while one was open for 3% -> 0% of each run, Pallas kernels for 0% -> 0%
where the time goes in v1:
time: 228 us; the launch traced here: 227 us
  Pallas kernels  218 us (96%)
  local copies, waits for them, and re-layouts  8.2 us (4%)
    pallas_call x1, Pallas kernels, local(): pl.pallas_call(functools.partial(kernel, n, groups, chunks, rate), out_sh...  218 us
    unnamed x8, local copies, waits for them, and re-layouts  8.2 us

profile of v1, /device:TPU:13, one launch (start us, length us, event | category | flops | bytes accessed | tf_op | source)
XLA Modules:
  0.0 227.1 jit_solution(17433608770433845424)
XLA Ops:
  0.6 218.2 %shard_map.93 = (bf16[256,512]{1,0:T(8,128)(2,1)}, bf16[256,8192]{1,0:T(8,128)(2,1)}, bf16[1024,512]{1,0:T(8,128)(2,1)}, f32[1024,128]{1,0:T(8,128)}) custom-call(s32[4]{0:T(128)} %plan.1, bf16[256,8192]{1,0:T(8,128)(2,1)} %bitcast.9, bf16[256,512]{1,0:T(8,128)(2,1)} %bitcast.11, bf16[1024,512]{1,0:T(8,128)(2,1)} %bitcast.10, f32[1024,128]{1,0:T(8,128)} %anchor_hbm.1, ...), custom_call_target="tpu_custom_call" | custom-call | flops 6442450944 | bytes 25165824 | tf_op jit(solution)/shard_map/pallas_call | solution.py:333
  218.9 1.7 copy.14
  220.6 0.0 copy-start
  220.6 0.0 copy-start.1
  220.6 4.8 %copy.15 = bf16[1,256,8192]{2,1,0:T(8,128)(2,1)} copy(bf16[1,256,8192]{2,1,0:T(8,128)(2,1)} %bitcast.6) | data formatting | bytes 8388608
  225.3 0.0 copy-done
  225.3 1.0 copy.16
  226.3 0.0 copy-done.1
  226.3 0.8 copy.17
Async XLA Ops:
  220.6 4.8 %copy-start = (bf16[1024,512]{1,0:T(8,128)(2,1)S(1)}, bf16[1024,512]{1,0:T(8,128)(2,1)}, u32[]{:S(2)}) copy-start(bf16[1024,512]{1,0:T(8,128)(2,1)} %get-tuple-element.10) | copy-start | bytes 3145732
  220.6 5.7 %copy-start.1 = (f32[1024,128]{1,0:T(8,128)S(1)}, f32[1024,128]{1,0:T(8,128)}, u32[]{:S(2)}) copy-start(f32[1024,128]{1,0:T(8,128)} %get-tuple-element.19) | copy-start | bytes 1572868

commit v2 on v1

--- a/solution.py
+++ b/solution.py
@@ -141,13 +141,13 @@
     load_og.wait()
     own(og_copy, start)
 
-    @pl.loop(1, n)
-    def _(k):
-        a_copy(k).start()
-
     for c in range(chunks):
         load_w(c).wait()
         own(w_copy(c), start)
+
+    @pl.loop(1, n)
+    def _(k):
+        a_copy(k).start()
 
     def ag_store(s):
         return pltpu.make_async_copy(ag.at[s], ag_hbm.at[:, cols(s)], ag_sem.at[s])
@@ -205,7 +205,11 @@
                     w_copy(c)(s, PARTNER).wait_recv()
                 use_weight(s)
 
-    gather(1)
+    ahead = max(line - 2, 1)
+
+    @pl.loop(1, ahead + 1)
+    def _(k):
+        gather(k)
 
     @pl.loop(0, line)
     def _(zz):
@@ -261,14 +265,16 @@
         r_copy(k).start()
     rep_in[rep] = inner[rep]
 
-    use_line(1)
+    @pl.loop(ahead + 1, line)
+    def _(k):
+        gather(k)
+
     use_partner(0)
 
-    @pl.loop(2, line)
-    def _(k):
-        gather(k)
+    @pl.loop(1, line - 1)
+    def _(k):
         use_line(k)
-        use_partner(k - 1)
+        use_partner(k)
 
     for k in range(1, groups):
         r_arrived(k).wait_recv()
@@ -287,6 +293,7 @@
     synced = jnp.full(mom_next.shape, plan[rep], jnp.int32) > 0
     new_mom_out[...] = jnp.where(synced, mom_next, mom[...])
 
+    use_line(line - 1)
     use_partner(line - 1)
     values_out[...] = vals[...].astype(BF16)
 

time: 228 us -> 228 us (level)
  no operation moved by 1% of the time
where the time goes in v2:
time: 228 us; the launch traced here: 227 us
  Pallas kernels  218 us (96%)
  local copies, waits for them, and re-layouts  8.2 us (4%)
    pallas_call x1, Pallas kernels, local(): pl.pallas_call(functools.partial(kernel, n, groups, chunks, rate), out_sh...  218 us
    unnamed x8, local copies, waits for them, and re-layouts  8.2 us

profile of v2, /device:TPU:13, one launch (start us, length us, event | category | flops | bytes accessed | tf_op | source)
XLA Modules:
  0.0 227.0 jit_solution(13065815030867523352)
XLA Ops:
  0.6 218.2 %shard_map.93 = (bf16[256,512]{1,0:T(8,128)(2,1)}, bf16[256,8192]{1,0:T(8,128)(2,1)}, bf16[1024,512]{1,0:T(8,128)(2,1)}, f32[1024,128]{1,0:T(8,128)}) custom-call(s32[4]{0:T(128)} %plan.1, bf16[256,8192]{1,0:T(8,128)(2,1)} %bitcast.9, bf16[256,512]{1,0:T(8,128)(2,1)} %bitcast.11, bf16[1024,512]{1,0:T(8,128)(2,1)} %bitcast.10, f32[1024,128]{1,0:T(8,128)} %anchor_hbm.1, ...), custom_call_target="tpu_custom_call" | custom-call | flops 6442450944 | bytes 25165824 | tf_op jit(solution)/shard_map/pallas_call | solution.py:340
  218.8 1.7 copy.14
  220.5 0.0 copy-start
  220.5 0.0 copy-start.1
  220.5 4.8 %copy.15 = bf16[1,256,8192]{2,1,0:T(8,128)(2,1)} copy(bf16[1,256,8192]{2,1,0:T(8,128)(2,1)} %bitcast.6) | data formatting | bytes 8388608
  225.3 0.0 copy-done
  225.3 1.0 copy.16
  226.2 0.0 copy-done.1
  226.3 0.8 copy.17
Async XLA Ops:
  220.5 4.8 %copy-start = (bf16[1024,512]{1,0:T(8,128)(2,1)S(1)}, bf16[1024,512]{1,0:T(8,128)(2,1)}, u32[]{:S(2)}) copy-start(bf16[1024,512]{1,0:T(8,128)(2,1)} %get-tuple-element.10) | copy-start | bytes 3145732
  220.5 5.7 %copy-start.1 = (f32[1024,128]{1,0:T(8,128)S(1)}, f32[1024,128]{1,0:T(8,128)}, u32[]{:S(2)}) copy-start(f32[1024,128]{1,0:T(8,128)} %get-tuple-element.19) | copy-start | bytes 1572868

commit v3 on v2

--- a/solution.py
+++ b/solution.py
@@ -145,9 +145,11 @@
         load_w(c).wait()
         own(w_copy(c), start)
 
-    @pl.loop(1, n)
-    def _(k):
-        a_copy(k).start()
+    def send_acts(near):
+        @pl.loop(1, n)
+        def _(k):
+            apart = jnp.abs(lax.rem(me + k, n) // 2 - z)
+            pl.when((apart == 1) == near)(lambda: a_copy(k).start())
 
     def ag_store(s):
         return pltpu.make_async_copy(ag.at[s], ag_hbm.at[:, cols(s)], ag_sem.at[s])
@@ -173,14 +175,11 @@
     def _(s):
         load_acts(s).wait()
 
-    @pl.loop(1, line)
-    def _(k):
-        forward(og_copy, k, start, True)
-
     use_weight(me)
     use_acts(acts[me], me)
 
     def gather(k):
+        forward(og_copy, k, start, True)
         for c in range(chunks):
             forward(w_copy(c), k, start, True)
 
@@ -205,11 +204,13 @@
                     w_copy(c)(s, PARTNER).wait_recv()
                 use_weight(s)
 
-    ahead = max(line - 2, 1)
-
-    @pl.loop(1, ahead + 1)
+    gather(1)
+    send_acts(False)
+
+    @pl.loop(2, line)
     def _(k):
         gather(k)
+        pl.when(k == 2)(lambda: send_acts(True))
 
     @pl.loop(0, line)
     def _(zz):
@@ -264,10 +265,6 @@
     for k in range(1, groups):
         r_copy(k).start()
     rep_in[rep] = inner[rep]
-
-    @pl.loop(ahead + 1, line)
-    def _(k):
-        gather(k)
 
     use_partner(0)
 

time: 228 us -> 213 us (0.934)
  the two profiles are of different devices: /device:TPU:13 before, /device:TPU:29 now
where the time goes in v3:
time: 213 us
  Pallas kernels  204 us (96%)
  local copies, waits for them, and re-layouts  8.2 us (4%)
    pallas_call x1, Pallas kernels, local(): pl.pallas_call(functools.partial(kernel, n, groups, chunks, rate), out_sh...  204 us
    unnamed x8, local copies, waits for them, and re-layouts  8.2 us

profile of v3, /device:TPU:29, one launch (start us, length us, event | category | flops | bytes accessed | tf_op | source)
XLA Modules:
  0.0 212.7 jit_solution(2878518340048403264)
XLA Ops:
  0.6 203.9 %shard_map.93 = (bf16[256,512]{1,0:T(8,128)(2,1)}, bf16[256,8192]{1,0:T(8,128)(2,1)}, bf16[1024,512]{1,0:T(8,128)(2,1)}, f32[1024,128]{1,0:T(8,128)}) custom-call(s32[4]{0:T(128)} %plan.1, bf16[256,8192]{1,0:T(8,128)(2,1)} %bitcast.9, bf16[256,512]{1,0:T(8,128)(2,1)} %bitcast.11, bf16[1024,512]{1,0:T(8,128)(2,1)} %bitcast.10, f32[1024,128]{1,0:T(8,128)} %anchor_hbm.1, ...), custom_call_target="tpu_custom_call" | custom-call | flops 6442450944 | bytes 25165824 | tf_op jit(solution)/shard_map/pallas_call | solution.py:337
  204.5 1.7 copy.14
  206.2 0.0 copy-start
  206.2 0.0 copy-start.1
  206.2 4.8 %copy.15 = bf16[1,256,8192]{2,1,0:T(8,128)(2,1)} copy(bf16[1,256,8192]{2,1,0:T(8,128)(2,1)} %bitcast.6) | data formatting | bytes 8388608
  210.9 0.0 copy-done
  210.9 1.0 copy.16
  211.9 0.0 copy-done.1
  211.9 0.8 copy.17
Async XLA Ops:
  206.2 4.8 %copy-start = (bf16[1024,512]{1,0:T(8,128)(2,1)S(1)}, bf16[1024,512]{1,0:T(8,128)(2,1)}, u32[]{:S(2)}) copy-start(bf16[1024,512]{1,0:T(8,128)(2,1)} %get-tuple-element.10) | copy-start | bytes 3145732
  206.2 5.7 %copy-start.1 = (f32[1024,128]{1,0:T(8,128)S(1)}, f32[1024,128]{1,0:T(8,128)}, u32[]{:S(2)}) copy-start(f32[1024,128]{1,0:T(8,128)} %get-tuple-element.19) | copy-start | bytes 1572868

commit v4 on v3

--- a/solution.py
+++ b/solution.py
@@ -20,7 +20,7 @@
     n, groups, chunks, rate,
     plan, acts_hbm, og_hbm, w_hbm, anchor_hbm, mom_hbm,
     values_out, ag_hbm, new_w_out, new_mom_out,
-    acts, acts_t, og_all, w_all, ag, vals, wgrad, inner, rep_in, outer_in, anchor, mom,
+    acts, acts_t, og_all, w_all, w_own, ag, vals, wgrad, inner, rep_in, outer_in, anchor, mom,
     acts_sem, og_sem, w_sem, state_sem, ag_sem,
     og_send, og_recv, w_send, w_recv, a_send, a_recv,
     r_send, r_recv, o_send, o_recv,
@@ -33,6 +33,7 @@
     width = acts.shape[2]
     rows = w_all.shape[2]
     block = anchor.shape[1]
+    parts, span = acts_t.shape[0], acts_t.shape[3]
 
     def cols(s):
         return pl.ds(pl.multiple_of(s * width, width), width)
@@ -56,6 +57,13 @@
     def _(s):
         load_acts(s).start()
 
+    def load_own(h):
+        return pltpu.make_async_copy(
+            w_hbm.at[pl.ds(h * span, span)], w_own.at[h], state_sem.at[2 + h]
+        )
+
+    for h in range(parts):
+        load_own(h).start()
     load_anchor.start()
     load_mom.start()
 
@@ -123,18 +131,21 @@
     def wait_send(copy):
         copy.wait_send()
 
-    def a_copy(k):
+    def piece(s, h):
+        return pl.ds(pl.multiple_of(s * width + h * span, span), span)
+
+    def a_copy(k, h):
         d = lax.rem(me + k, n)
         return pltpu.make_async_remote_copy(
-            src_ref=acts_hbm.at[:, cols(d)], dst_ref=acts_t.at[me],
-            send_sem=a_send.at[k], recv_sem=a_recv.at[me],
+            src_ref=acts_hbm.at[:, piece(d, h)], dst_ref=acts_t.at[h, me],
+            send_sem=a_send.at[k, h], recv_sem=a_recv.at[me, h],
             device_id={"fsdp": d}, device_id_type=MESH,
         )
 
-    def a_arrived(s):
-        return pltpu.make_async_remote_copy(
-            src_ref=acts_hbm.at[:, cols(s)], dst_ref=acts_t.at[s],
-            send_sem=a_send.at[0], recv_sem=a_recv.at[s],
+    def a_arrived(s, h):
+        return pltpu.make_async_remote_copy(
+            src_ref=acts_hbm.at[:, piece(s, h)], dst_ref=acts_t.at[h, s],
+            send_sem=a_send.at[0, h], recv_sem=a_recv.at[s, h],
             device_id={"fsdp": lax.rem(me + 1, n)}, device_id_type=MESH,
         )
 
@@ -145,11 +156,11 @@
         load_w(c).wait()
         own(w_copy(c), start)
 
-    def send_acts(near):
-        @pl.loop(1, n)
-        def _(k):
-            apart = jnp.abs(lax.rem(me + k, n) // 2 - z)
-            pl.when((apart == 1) == near)(lambda: a_copy(k).start())
+    def send_acts(first, last):
+        for h in range(first, last):
+            @pl.loop(1, n)
+            def _(k):
+                a_copy(k, h).start()
 
     def ag_store(s):
         return pltpu.make_async_copy(ag.at[s], ag_hbm.at[:, cols(s)], ag_sem.at[s])
@@ -163,8 +174,8 @@
             ).astype(BF16)
         ag_store(s).start()
 
-    def use_acts(a, s):
-        wgrad[...] += lax.dot_general(
+    def use_acts(a, s, h):
+        wgrad[h] += lax.dot_general(
             a, og_all[s], (((0,), (0,)), ((), ())), preferred_element_type=F32
         )
 
@@ -176,7 +187,8 @@
         load_acts(s).wait()
 
     use_weight(me)
-    use_acts(acts[me], me)
+    for h in range(parts):
+        use_acts(acts[me, :, h * span:(h + 1) * span], me, h)
 
     def gather(k):
         forward(og_copy, k, start, True)
@@ -205,67 +217,98 @@
                 use_weight(s)
 
     gather(1)
-    send_acts(False)
+    send_acts(0, (parts + 1) // 2)
 
     @pl.loop(2, line)
     def _(k):
         gather(k)
-        pl.when(k == 2)(lambda: send_acts(True))
+        pl.when(k == 2)(lambda: send_acts((parts + 1) // 2, parts))
 
     @pl.loop(0, line)
     def _(zz):
         og_copy(zz * 2 + 1 - y, PARTNER).wait_recv()
 
-    @pl.loop(1, n)
-    def _(k):
-        s = lax.rem(me + n - k, n)
-        a_arrived(s).wait_recv()
-        use_acts(acts_t[s], s)
-
-    for j in range(groups):
-        part = slice(j * block, (j + 1) * block)
-        for c in range(chunks):
-            across = slice(c * rows, (c + 1) * rows)
-            inner[j, across] = (
-                w_all[me, c, :, part].astype(F32) - rate * wgrad[across, part]
-            )
-
-    def r_copy(k):
+    def r_copy(k, h):
         d = lax.rem(rep + k, groups)
         return pltpu.make_async_remote_copy(
-            src_ref=inner.at[d], dst_ref=rep_in.at[rep],
-            send_sem=r_send.at[k], recv_sem=r_recv.at[rep],
+            src_ref=inner.at[h, d], dst_ref=rep_in.at[h, rep],
+            send_sem=r_send.at[k, h], recv_sem=r_recv.at[rep, h],
             device_id={"rep": d}, device_id_type=MESH,
         )
 
-    def r_arrived(k):
+    def r_arrived(k, h):
         d = lax.rem(rep + k, groups)
         return pltpu.make_async_remote_copy(
-            src_ref=inner.at[d], dst_ref=rep_in.at[d],
-            send_sem=r_send.at[k], recv_sem=r_recv.at[d],
+            src_ref=inner.at[h, d], dst_ref=rep_in.at[h, d],
+            send_sem=r_send.at[k, h], recv_sem=r_recv.at[d, h],
             device_id={"rep": d}, device_id_type=MESH,
         )
 
-    def o_copy(k):
+    def o_copy(k, h):
         d = lax.rem(rep + k, groups)
         return pltpu.make_async_remote_copy(
-            src_ref=outer_in.at[rep], dst_ref=outer_in.at[rep],
-            send_sem=o_send.at[k], recv_sem=o_recv.at[rep],
+            src_ref=outer_in.at[h, rep], dst_ref=outer_in.at[h, rep],
+            send_sem=o_send.at[k, h], recv_sem=o_recv.at[rep, h],
             device_id={"rep": d}, device_id_type=MESH,
         )
 
-    def o_arrived(k):
+    def o_arrived(k, h):
         d = lax.rem(rep + k, groups)
         return pltpu.make_async_remote_copy(
-            src_ref=outer_in.at[d], dst_ref=outer_in.at[d],
-            send_sem=o_send.at[k], recv_sem=o_recv.at[d],
+            src_ref=outer_in.at[h, d], dst_ref=outer_in.at[h, d],
+            send_sem=o_send.at[k, h], recv_sem=o_recv.at[d, h],
             device_id={"rep": d}, device_id_type=MESH,
         )
 
-    for k in range(1, groups):
-        r_copy(k).start()
-    rep_in[rep] = inner[rep]
-
+    def inner_step(h):
+        @pl.loop(1, n)
+        def _(k):
+            s = lax.rem(me + n - k, n)
+            a_arrived(s, h).wait_recv()
+            use_acts(acts_t[h, s], s, h)
+
+        for j in range(groups):
+            part = slice(j * block, (j + 1) * block)
+            inner[h, j] = w_own[h, :, part].astype(F32) - rate * wgrad[h, :, part]
+        for k in range(1, groups):
+            r_copy(k, h).start()
+        rep_in[h, rep] = inner[h, rep]
+
+    def outer_step(h):
+        across = slice(h * span, (h + 1) * span)
+        for k in range(1, groups):
+            r_arrived(k, h).wait_recv()
+        total = rep_in[h, 0]
+        for j in range(1, groups):
+            total = total + rep_in[h, j]
+        pseudo_grad = anchor[across] - total / groups
+        mom_next = momentum_coef * mom[across] + pseudo_grad
+        outer_in[h, rep] = (
+            anchor[across] - outer_rate * (pseudo_grad + momentum_coef * mom_next)
+        ).astype(BF16)
+        for k in range(1, groups):
+            o_copy(k, h).start()
+        synced = jnp.full(mom_next.shape, plan[rep], jnp.int32) > 0
+        new_mom_out[across] = jnp.where(synced, mom_next, mom[across])
+
+    def last_step(h):
+        across = slice(h * span, (h + 1) * span)
+        for k in range(1, groups):
+            o_arrived(k, h).wait_recv()
+        for j in range(groups):
+            synced = jnp.full(inner.shape[2:], plan[j], jnp.int32) > 0
+            new_w_out[across, j * block:(j + 1) * block] = jnp.where(
+                synced, outer_in[h, j].astype(F32), inner[h, j]
+            ).astype(BF16)
+
+    load_anchor.wait()
+    load_mom.wait()
+    for c in range(parts):
+        load_own(c).wait()
+    inner_step(0)
+    for h in range(1, parts):
+        inner_step(h)
+        outer_step(h - 1)
     use_partner(0)
 
     @pl.loop(1, line - 1)
@@ -273,34 +316,13 @@
         use_line(k)
         use_partner(k)
 
-    for k in range(1, groups):
-        r_arrived(k).wait_recv()
-    load_anchor.wait()
-    load_mom.wait()
-    total = rep_in[0]
-    for j in range(1, groups):
-        total = total + rep_in[j]
-    pseudo_grad = anchor[...] - total / groups
-    mom_next = momentum_coef * mom[...] + pseudo_grad
-    outer_in[rep] = (
-        anchor[...] - outer_rate * (pseudo_grad + momentum_coef * mom_next)
-    ).astype(BF16)
-    for k in range(1, groups):
-        o_copy(k).start()
-    synced = jnp.full(mom_next.shape, plan[rep], jnp.int32) > 0
-    new_mom_out[...] = jnp.where(synced, mom_next, mom[...])
-
     use_line(line - 1)
+    outer_step(parts - 1)
+    for h in range(parts - 1):
+        last_step(h)
     use_partner(line - 1)
     values_out[...] = vals[...].astype(BF16)
-
-    for k in range(1, groups):
-        o_arrived(k).wait_recv()
-    for j in range(groups):
-        synced = jnp.full(inner.shape[1:], plan[j], jnp.int32) > 0
-        new_w_out[:, j * block:(j + 1) * block] = jnp.where(
-            synced, outer_in[j].astype(F32), inner[j]
-        ).astype(BF16)
+    last_step(parts - 1)
 
     own(og_copy, wait_send)
     for c in range(chunks):
@@ -314,11 +336,13 @@
 
     @pl.loop(1, n)
     def _(k):
-        a_copy(k).wait_send()
+        for h in range(parts):
+            a_copy(k, h).wait_send()
 
     for k in range(1, groups):
-        r_copy(k).wait_send()
-        o_copy(k).wait_send()
+        for h in range(parts):
+            r_copy(k, h).wait_send()
+            o_copy(k, h).wait_send()
 
     @pl.loop(0, n)
     def _(s):
@@ -330,7 +354,8 @@
     rows, kvw = weights.shape[1:]
     block = anchor.shape[1]
     rate = 1.0 / math.sqrt(tokens * n * depth)
-    chunks = 2
+    parts = chunks = max(1, min(4, rows // 256))
+    span = rows // parts
     any_spec = pl.BlockSpec(memory_space=pl.ANY)
     vmem = pl.BlockSpec(memory_space=pltpu.VMEM)
     dma = pltpu.SemaphoreType.DMA
@@ -346,20 +371,22 @@
         out_specs=(vmem, any_spec, vmem, vmem),
         scratch_shapes=[
             pltpu.VMEM((n, tokens, rows), BF16),
-            pltpu.VMEM((n, tokens, rows), BF16),
+            pltpu.VMEM((parts, n, tokens, span), BF16),
             pltpu.VMEM((n, tokens, kvw), BF16),
             pltpu.VMEM((n, chunks, rows // chunks, kvw), BF16),
+            pltpu.VMEM((parts, span, kvw), BF16),
             pltpu.VMEM((n, tokens, rows), BF16),
             pltpu.VMEM((tokens, kvw), F32),
-            pltpu.VMEM((rows, kvw), F32),
-            pltpu.VMEM((groups, rows, block), F32),
-            pltpu.VMEM((groups, rows, block), F32),
-            pltpu.VMEM((groups, rows, block), BF16),
+            pltpu.VMEM((parts, span, kvw), F32),
+            pltpu.VMEM((parts, groups, span, block), F32),
+            pltpu.VMEM((parts, groups, span, block), F32),
+            pltpu.VMEM((parts, groups, span, block), BF16),
             pltpu.VMEM((rows, block), F32),
             pltpu.VMEM((rows, block), F32),
-            dma((n,)), dma((1,)), dma((chunks,)), dma((2,)), dma((n,)),
-            dma((n, 3)), dma((n,)), dma((n, chunks, 3)), dma((n, chunks)), dma((n,)), dma((n,)),
-            dma((groups,)), dma((groups,)), dma((groups,)), dma((groups,)),
+            dma((n,)), dma((1,)), dma((chunks,)), dma((2 + parts,)), dma((n,)),
+            dma((n, 3)), dma((n,)), dma((n, chunks, 3)), dma((n, chunks)),
+            dma((n, parts)), dma((n, parts)),
+            dma((groups, parts)), dma((groups, parts)), dma((groups, parts)), dma((groups, parts)),
         ],
         compiler_params=pltpu.CompilerParams(
             collective_id=0, has_side_effects=True, vmem_limit_bytes=56 * 2**20

time: 213 us -> 196 us (0.920)
  the two profiles are of different devices: /device:TPU:29 before, /device:TPU:13 now
where the time goes in v4:
time: 196 us
  Pallas kernels  187 us (95%)
  local copies, waits for them, and re-layouts  8.2 us (4%)
    pallas_call x1, Pallas kernels, local(): pl.pallas_call(functools.partial(kernel, n, groups, chunks, rate), out_sh...  187 us
    unnamed x8, local copies, waits for them, and re-layouts  8.2 us

profile of v4, /device:TPU:13, one launch (start us, length us, event | category | flops | bytes accessed | tf_op | source)
XLA Modules:
  0.0 195.8 jit_solution(10839886043230448397)
XLA Ops:
  0.6 186.9 %shard_map.93 = (bf16[256,512]{1,0:T(8,128)(2,1)}, bf16[256,8192]{1,0:T(8,128)(2,1)}, bf16[1024,512]{1,0:T(8,128)(2,1)}, f32[1024,128]{1,0:T(8,128)}) custom-call(s32[4]{0:T(128)} %plan.1, bf16[256,8192]{1,0:T(8,128)(2,1)} %bitcast.9, bf16[256,512]{1,0:T(8,128)(2,1)} %bitcast.11, bf16[1024,512]{1,0:T(8,128)(2,1)} %bitcast.10, f32[1024,128]{1,0:T(8,128)} %anchor_hbm.1, ...), custom_call_target="tpu_custom_call" | custom-call | flops 6442450944 | bytes 25165824 | tf_op jit(solution)/shard_map/pallas_call | solution.py:362
  187.6 1.7 copy.14
  189.3 0.0 copy-start
  189.3 0.0 copy-start.1
  189.3 4.8 %copy.15 = bf16[1,256,8192]{2,1,0:T(8,128)(2,1)} copy(bf16[1,256,8192]{2,1,0:T(8,128)(2,1)} %bitcast.6) | data formatting | bytes 8388608
  194.0 0.0 copy-done
  194.0 1.0 copy.16
  195.0 0.0 copy-done.1
  195.0 0.8 copy.17
Async XLA Ops:
  189.3 4.8 %copy-start = (bf16[1024,512]{1,0:T(8,128)(2,1)S(1)}, bf16[1024,512]{1,0:T(8,128)(2,1)}, u32[]{:S(2)}) copy-start(bf16[1024,512]{1,0:T(8,128)(2,1)} %get-tuple-element.10) | copy-start | bytes 3145732
  189.3 5.7 %copy-start.1 = (f32[1024,128]{1,0:T(8,128)S(1)}, f32[1024,128]{1,0:T(8,128)}, u32[]{:S(2)}) copy-start(f32[1024,128]{1,0:T(8,128)} %get-tuple-element.19) | copy-start | bytes 1572868

commit v5 on v4

--- a/solution.py
+++ b/solution.py
@@ -218,11 +218,14 @@
 
     gather(1)
     send_acts(0, (parts + 1) // 2)
+    use_partner(0)
 
     @pl.loop(2, line)
     def _(k):
         gather(k)
         pl.when(k == 2)(lambda: send_acts((parts + 1) // 2, parts))
+        use_line(k - 1)
+        use_partner(k - 1)
 
     @pl.loop(0, line)
     def _(zz):
@@ -309,13 +312,6 @@
     for h in range(1, parts):
         inner_step(h)
         outer_step(h - 1)
-    use_partner(0)
-
-    @pl.loop(1, line - 1)
-    def _(k):
-        use_line(k)
-        use_partner(k)
-
     use_line(line - 1)
     outer_step(parts - 1)
     for h in range(parts - 1):
@@ -357,6 +353,11 @@
     parts = chunks = max(1, min(4, rows // 256))
     span = rows // parts
     any_spec = pl.BlockSpec(memory_space=pl.ANY)
+    hbm = pl.BlockSpec(memory_space=pltpu.HBM)
+    held = (
+        6 * n * tokens * rows + 2 * n * (tokens + rows) * kvw + 6 * tokens * kvw
+        + 18 * rows * kvw + 12 * rows * block
+    )
     vmem = pl.BlockSpec(memory_space=pltpu.VMEM)
     dma = pltpu.SemaphoreType.DMA
     values, act_grad, new_w, new_mom = pl.pallas_call(
@@ -367,7 +368,7 @@
             jax.ShapeDtypeStruct((rows, kvw), BF16),
             jax.ShapeDtypeStruct((rows, block), F32),
         ),
-        in_specs=[pl.BlockSpec(memory_space=pltpu.SMEM)] + [any_spec] * 5,
+        in_specs=[pl.BlockSpec(memory_space=pltpu.SMEM)] + [hbm] * 5,
         out_specs=(vmem, any_spec, vmem, vmem),
         scratch_shapes=[
             pltpu.VMEM((n, tokens, rows), BF16),
@@ -389,7 +390,7 @@
             dma((groups, parts)), dma((groups, parts)), dma((groups, parts)), dma((groups, parts)),
         ],
         compiler_params=pltpu.CompilerParams(
-            collective_id=0, has_side_effects=True, vmem_limit_bytes=56 * 2**20
+            collective_id=0, has_side_effects=True, vmem_limit_bytes=held + 4 * 2**20
         ),
         cost_estimate=pl.CostEstimate(
             flops=6 * tokens * depth * kvw, bytes_accessed=24 * 2**20, transcendentals=0

time: 196 us -> 211 us (1.077)
  Pallas kernels: 187 us -> 198 us
  local copies, waits for them, and re-layouts: 8.2 us -> 11.6 us
    pallas_call x1, Pallas kernels: 187 us -> 198 us  [local(): pl.pallas_call(functools.partial(kernel, n, groups, chunks, rate), out_sh...]
    unnamed x8 -> x16, local copies, waits for them, and re-layouts: 8.2 us -> 11.6 us
where the time goes in v5:
time: 211 us; the launch traced here: 210 us
  Pallas kernels  198 us (94%)
  local copies, waits for them, and re-layouts  11.6 us (5%)
    pallas_call x1, Pallas kernels, local(): pl.pallas_call(functools.partial(kernel, n, groups, chunks, rate), out_sh...  198 us
    unnamed x16, local copies, waits for them, and re-layouts  11.6 us

profile of v5, /device:TPU:13, one launch (start us, length us, event | category | flops | bytes accessed | tf_op | source)
XLA Modules:
  0.0 210.3 jit_solution(2689973562699947877)
XLA Ops:
  0.6 0.0 copy-start
  0.6 2.2 %copy-done = bf16[1,256,8192]{2,1,0:T(8,128)(2,1)S(1)} copy-done((bf16[1,256,8192]{2,1,0:T(8,128)(2,1)S(1)}, bf16[1,256,8192]{2,1,0:T(8,128)(2,1)}, u32[]{:S(2)}) %copy-start) | copy-done | bytes 4194328
  2.8 0.0 copy-start.1
  2.8 1.2 copy-done.1
  4.0 0.0 copy-start.2
  4.0 1.0 copy-done.2
  5.1 0.0 copy-start.3
  5.1 1.0 copy-done.3
  6.1 0.0 copy-start.4
  6.1 0.9 copy-done.4
  7.1 0.0 copy-start.5
  7.1 0.7 copy-done.5
  7.7 198.1 %shard_map.93 = (bf16[256,512]{1,0:T(8,128)(2,1)S(1)}, bf16[256,8192]{1,0:T(8,128)(2,1)S(1)}, bf16[1024,512]{1,0:T(8,128)(2,1)S(1)}, f32[1024,128]{1,0:T(8,128)S(1)}) custom-call(s32[4]{0:T(128)S(1)} %copy-done.5, bf16[256,8192]{1,0:T(8,128)(2,1)S(1)} %bitcast.9, bf16[256,512]{1,0:T(8,128)(2,1)S(1)} %bitcast.11, bf16[1024,512]{1,0:T(8,128)(2,1)S(1)} %bitcast.10, ...), custom_call_target="tpu_custom_call" | custom-call | flops 6442450944 | bytes 25165824 | tf_op jit(solution)/shard_map/pallas_call | solution.py:363
  205.9 0.7 copy.14
  206.6 2.0 copy.15
  208.6 1.0 copy.16
  209.6 0.8 copy.17
Async XLA Ops:
  0.6 2.2 %copy-start = (bf16[1,256,8192]{2,1,0:T(8,128)(2,1)S(1)}, bf16[1,256,8192]{2,1,0:T(8,128)(2,1)}, u32[]{:S(2)}) copy-start(bf16[1,256,8192]{2,1,0:T(8,128)(2,1)} %param.6) | copy-start | bytes 12582916
  2.8 1.2 copy-start.1
  4.0 1.0 copy-start.2
  5.1 1.0 copy-start.3
  6.1 0.9 copy-start.4
  7.1 0.7 copy-start.5

commit v6 on v4

--- a/solution.py
+++ b/solution.py
@@ -134,8 +134,10 @@
     def piece(s, h):
         return pl.ds(pl.multiple_of(s * width + h * span, span), span)
 
+    toward = 1 - 2 * (z // (line // 2))
+
     def a_copy(k, h):
-        d = lax.rem(me + k, n)
+        d = lax.rem(me + toward * k + n, n)
         return pltpu.make_async_remote_copy(
             src_ref=acts_hbm.at[:, piece(d, h)], dst_ref=acts_t.at[h, me],
             send_sem=a_send.at[k, h], recv_sem=a_recv.at[me, h],
@@ -160,7 +162,7 @@
         for h in range(first, last):
             @pl.loop(1, n)
             def _(k):
-                a_copy(k, h).start()
+                a_copy(n - k, h).start()
 
     def ag_store(s):
         return pltpu.make_async_copy(ag.at[s], ag_hbm.at[:, cols(s)], ag_sem.at[s])
@@ -223,6 +225,11 @@
     def _(k):
         gather(k)
         pl.when(k == 2)(lambda: send_acts((parts + 1) // 2, parts))
+
+        @pl.when(k == 2)
+        def _():
+            use_partner(0)
+            use_line(1)
 
     @pl.loop(0, line)
     def _(zz):
@@ -309,9 +316,12 @@
     for h in range(1, parts):
         inner_step(h)
         outer_step(h - 1)
-    use_partner(0)
-
-    @pl.loop(1, line - 1)
+        if h == 1:
+            use_partner(1)
+    if parts == 1:
+        use_partner(1)
+
+    @pl.loop(2, line - 1)
     def _(k):
         use_line(k)
         use_partner(k)

time: 196 us -> 196 us (level)
  no operation moved by 1% of the time
where the time goes in v6:
time: 196 us
  Pallas kernels  187 us (95%)
  local copies, waits for them, and re-layouts  8.2 us (4%)
    pallas_call x1, Pallas kernels, local(): pl.pallas_call(functools.partial(kernel, n, groups, chunks, rate), out_sh...  187 us
    unnamed x8, local copies, waits for them, and re-layouts  8.2 us

profile of v6, /device:TPU:13, one launch (start us, length us, event | category | flops | bytes accessed | tf_op | source)
XLA Modules:
  0.0 195.8 jit_solution(13453666322570218714)
XLA Ops:
  0.6 186.9 %shard_map.93 = (bf16[256,512]{1,0:T(8,128)(2,1)}, bf16[256,8192]{1,0:T(8,128)(2,1)}, bf16[1024,512]{1,0:T(8,128)(2,1)}, f32[1024,128]{1,0:T(8,128)}) custom-call(s32[4]{0:T(128)} %plan.1, bf16[256,8192]{1,0:T(8,128)(2,1)} %bitcast.9, bf16[256,512]{1,0:T(8,128)(2,1)} %bitcast.11, bf16[1024,512]{1,0:T(8,128)(2,1)} %bitcast.10, f32[1024,128]{1,0:T(8,128)} %anchor_hbm.1, ...), custom_call_target="tpu_custom_call" | custom-call | flops 6442450944 | bytes 25165824 | tf_op jit(solution)/shard_map/pallas_call | solution.py:372
  187.6 1.7 copy.14
  189.3 0.0 copy-start
  189.3 0.0 copy-start.1
  189.3 4.8 %copy.15 = bf16[1,256,8192]{2,1,0:T(8,128)(2,1)} copy(bf16[1,256,8192]{2,1,0:T(8,128)(2,1)} %bitcast.6) | data formatting | bytes 8388608
  194.0 0.0 copy-done
  194.0 1.0 copy.16
  195.0 0.0 copy-done.1
  195.0 0.8 copy.17
Async XLA Ops:
  189.3 4.8 %copy-start = (bf16[1024,512]{1,0:T(8,128)(2,1)S(1)}, bf16[1024,512]{1,0:T(8,128)(2,1)}, u32[]{:S(2)}) copy-start(bf16[1024,512]{1,0:T(8,128)(2,1)} %get-tuple-element.10) | copy-start | bytes 3145732
  189.3 5.7 %copy-start.1 = (f32[1024,128]{1,0:T(8,128)S(1)}, f32[1024,128]{1,0:T(8,128)}, u32[]{:S(2)}) copy-start(f32[1024,128]{1,0:T(8,128)} %get-tuple-element.19) | copy-start | bytes 1572868

commit v7 on v6

--- a/solution.py
+++ b/solution.py
@@ -158,11 +158,10 @@
         load_w(c).wait()
         own(w_copy(c), start)
 
-    def send_acts(first, last):
-        for h in range(first, last):
-            @pl.loop(1, n)
-            def _(k):
-                a_copy(n - k, h).start()
+    def send_acts(h):
+        @pl.loop(1, n)
+        def _(k):
+            a_copy(n - k, h).start()
 
     def ag_store(s):
         return pltpu.make_async_copy(ag.at[s], ag_hbm.at[:, cols(s)], ag_sem.at[s])
@@ -217,23 +216,6 @@
                 for c in range(chunks):
                     w_copy(c)(s, PARTNER).wait_recv()
                 use_weight(s)
-
-    gather(1)
-    send_acts(0, (parts + 1) // 2)
-
-    @pl.loop(2, line)
-    def _(k):
-        gather(k)
-        pl.when(k == 2)(lambda: send_acts((parts + 1) // 2, parts))
-
-        @pl.when(k == 2)
-        def _():
-            use_partner(0)
-            use_line(1)
-
-    @pl.loop(0, line)
-    def _(zz):
-        og_copy(zz * 2 + 1 - y, PARTNER).wait_recv()
 
     def r_copy(k, h):
         d = lax.rem(rep + k, groups)
@@ -310,16 +292,38 @@
 
     load_anchor.wait()
     load_mom.wait()
-    for c in range(parts):
-        load_own(c).wait()
-    inner_step(0)
-    for h in range(1, parts):
+    for h in range(parts):
+        load_own(h).wait()
+
+    gather(1)
+    send_acts(0)
+
+    @pl.loop(2, line - 1)
+    def _(k):
+        gather(k)
+
+    if parts > 1:
+        send_acts(1)
+    use_line(1)
+    use_partner(0)
+
+    forward(og_copy, line - 1, start, True)
+
+    @pl.loop(0, line)
+    def _(zz):
+        og_copy(zz * 2 + 1 - y, PARTNER).wait_recv()
+
+    for h in range(parts):
         inner_step(h)
-        outer_step(h - 1)
-        if h == 1:
+        if h + 2 < parts:
+            send_acts(h + 2)
+        if h == 0:
+            for c in range(chunks):
+                forward(w_copy(c), line - 1, start, True)
+        if h > 0:
+            outer_step(h - 1)
+        if h == min(1, parts - 1):
             use_partner(1)
-    if parts == 1:
-        use_partner(1)
 
     @pl.loop(2, line - 1)
     def _(k):

time: 196 us -> 199 us (1.015)
  Pallas kernels: 187 us -> 190 us
    pallas_call x1, Pallas kernels: 187 us -> 190 us  [local(): pl.pallas_call(functools.partial(kernel, n, groups, chunks, rate), out_sh...]
where the time goes in v7:
time: 199 us
  Pallas kernels  190 us (95%)
  local copies, waits for them, and re-layouts  8.2 us (4%)
    pallas_call x1, Pallas kernels, local(): pl.pallas_call(functools.partial(kernel, n, groups, chunks, rate), out_sh...  190 us
    unnamed x8, local copies, waits for them, and re-layouts  8.2 us

profile of v7, /device:TPU:13, one launch (start us, length us, event | category | flops | bytes accessed | tf_op | source)
XLA Modules:
  0.0 198.6 jit_solution(12482112036087149430)
XLA Ops:
  0.6 189.8 %shard_map.93 = (bf16[256,512]{1,0:T(8,128)(2,1)}, bf16[256,8192]{1,0:T(8,128)(2,1)}, bf16[1024,512]{1,0:T(8,128)(2,1)}, f32[1024,128]{1,0:T(8,128)}) custom-call(s32[4]{0:T(128)} %plan.1, bf16[256,8192]{1,0:T(8,128)(2,1)} %bitcast.9, bf16[256,512]{1,0:T(8,128)(2,1)} %bitcast.11, bf16[1024,512]{1,0:T(8,128)(2,1)} %bitcast.10, f32[1024,128]{1,0:T(8,128)} %anchor_hbm.1, ...), custom_call_target="tpu_custom_call" | custom-call | flops 6442450944 | bytes 25165824 | tf_op jit(solution)/shard_map/pallas_call | solution.py:376
  190.4 1.7 copy.14
  192.1 0.0 copy-start
  192.1 0.0 copy-start.1
  192.1 4.8 %copy.15 = bf16[1,256,8192]{2,1,0:T(8,128)(2,1)} copy(bf16[1,256,8192]{2,1,0:T(8,128)(2,1)} %bitcast.6) | data formatting | bytes 8388608
  196.8 0.0 copy-done
  196.8 1.0 copy.16
  197.8 0.0 copy-done.1
  197.8 0.8 copy.17
Async XLA Ops:
  192.1 4.8 %copy-start = (bf16[1024,512]{1,0:T(8,128)(2,1)S(1)}, bf16[1024,512]{1,0:T(8,128)(2,1)}, u32[]{:S(2)}) copy-start(bf16[1024,512]{1,0:T(8,128)(2,1)} %get-tuple-element.10) | copy-start | bytes 3145732
  192.1 5.7 %copy-start.1 = (f32[1024,128]{1,0:T(8,128)S(1)}, f32[1024,128]{1,0:T(8,128)}, u32[]{:S(2)}) copy-start(f32[1024,128]{1,0:T(8,128)} %get-tuple-element.19) | copy-start | bytes 1572868

commit v8 on v4

--- a/solution.py
+++ b/solution.py
@@ -354,7 +354,8 @@
     rows, kvw = weights.shape[1:]
     block = anchor.shape[1]
     rate = 1.0 / math.sqrt(tokens * n * depth)
-    parts = chunks = max(1, min(4, rows // 256))
+    parts = max(1, min(8, rows // 128))
+    chunks = max(1, min(4, rows // 256))
     span = rows // parts
     any_spec = pl.BlockSpec(memory_space=pl.ANY)
     vmem = pl.BlockSpec(memory_space=pltpu.VMEM)

time: 196 us -> 197 us (level); the launches traced: 196 us -> 195 us
  no operation moved by 1% of the time
where the time goes in v8:
time: 197 us; the launch traced here: 195 us
  Pallas kernels  186 us (94%)
  local copies, waits for them, and re-layouts  8.2 us (4%)
    pallas_call x1, Pallas kernels, local(): pl.pallas_call(functools.partial(kernel, n, groups, chunks, rate), out_sh...  186 us
    unnamed x8, local copies, waits for them, and re-layouts  8.2 us

profile of v8, /device:TPU:13, one launch (start us, length us, event | category | flops | bytes accessed | tf_op | source)
XLA Modules:
  0.0 194.7 jit_solution(17039851245177940451)
XLA Ops:
  0.6 185.9 %shard_map.93 = (bf16[256,512]{1,0:T(8,128)(2,1)}, bf16[256,8192]{1,0:T(8,128)(2,1)}, bf16[1024,512]{1,0:T(8,128)(2,1)}, f32[1024,128]{1,0:T(8,128)}) custom-call(s32[4]{0:T(128)} %plan.1, bf16[256,8192]{1,0:T(8,128)(2,1)} %bitcast.9, bf16[256,512]{1,0:T(8,128)(2,1)} %bitcast.11, bf16[1024,512]{1,0:T(8,128)(2,1)} %bitcast.10, f32[1024,128]{1,0:T(8,128)} %anchor_hbm.1, ...), custom_call_target="tpu_custom_call" | custom-call | flops 6442450944 | bytes 25165824 | tf_op jit(solution)/shard_map/pallas_call | solution.py:363
  186.5 1.7 copy.14
  188.2 0.0 copy-start
  188.2 0.0 copy-start.1
  188.2 4.8 %copy.15 = bf16[1,256,8192]{2,1,0:T(8,128)(2,1)} copy(bf16[1,256,8192]{2,1,0:T(8,128)(2,1)} %bitcast.6) | data formatting | bytes 8388608
  193.0 0.0 copy-done
  193.0 1.0 copy.16
  194.0 0.0 copy-done.1
  194.0 0.8 copy.17
Async XLA Ops:
  188.2 4.8 %copy-start = (bf16[1024,512]{1,0:T(8,128)(2,1)S(1)}, bf16[1024,512]{1,0:T(8,128)(2,1)}, u32[]{:S(2)}) copy-start(bf16[1024,512]{1,0:T(8,128)(2,1)} %get-tuple-element.10) | copy-start | bytes 3145732
  188.2 5.7 %copy-start.1 = (f32[1024,128]{1,0:T(8,128)S(1)}, f32[1024,128]{1,0:T(8,128)}, u32[]{:S(2)}) copy-start(f32[1024,128]{1,0:T(8,128)} %get-tuple-element.19) | copy-start | bytes 1572868
